TPU v7x, 256 devices: a whole 4x4x8 slice. The times are simulated.
256 devices in a mesh: wide: 16 (over z, x_hi), narrow: 16 (over y, x_lo, core).
Axes of the slice: x: 4 (x_hi: 2, x_lo: 2; x = x_hi * 2 + x_lo), y: 4, z: 8, core: 2. Of those that a mesh axis runs over, the one named last changes fastest.
Arguments:
- states: bfloat16 [256, 2097152], P('narrow', 'wide'), may hold values from -6 to 6
- obs_ens: bfloat16 [256, 65536], P('narrow', 'wide'), may hold values from -6 to 6
- obs_value: float32 [65536], P('wide'), may hold values from -6 to 6
- obs_prec: float32 [65536], P('wide'), may hold values from 0.1 to 1
- obs_pick: int32 [256, 1024], P('wide'), may hold values from 0 to 4607, as said below
- taper: float32 [256, 1024], P(('wide', 'narrow')), may hold values from 0.1 to 1
Outputs:
- analysis: bfloat16 [256, 2097152], P('narrow', 'wide')
Inputs may be any that keep to these rules, and one draw needn't show every extreme that they name: `obs_pick`: within a region the 1024 rows are distinct.
All inputs are finite; a program needn't handle non-finite values.
Results may differ from a plain program's by a relative error of at most 0.0057.
Values may be sent and summed in bfloat16 or wider, within the bound.
A program may use at most 64 MiB of HBM per device.

v0:
```python
import jax
import jax.numpy as jnp
from jax import lax
from jax.sharding import PartitionSpec as P

HALO = 256
ITERS = 6


def padded(array, sides, width):
    for axis, dim in sides:
        size, length = (lax.axis_size(axis), array.shape[dim])
        up = [(i, (i + 1) % size) for i in range(size)]
        down = [(j, i) for i, j in up]
        last = lax.slice_in_dim(array, length - width, length, axis=dim)
        leading = lax.slice_in_dim(array, 0, width, axis=dim)
        before = lax.ppermute(last, axis, up)
        after = lax.ppermute(leading, axis, down)
        array = jnp.concatenate([before, array, after], axis=dim)
    return array


def analyse(ensemble, observed, precision, taper_row, regional):
    members = ensemble.shape[0]
    obs_mean = jnp.mean(ensemble, axis=0)
    obs_pert = ensemble - obs_mean
    obs_weight = precision * taper_row
    scaled = (obs_pert * jnp.sqrt(obs_weight)).astype(jnp.bfloat16)
    identity = jnp.eye(members, dtype=jnp.float32)
    gram_sum = lax.dot_general(
        scaled, scaled, (((1,), (1,)), ((), ())), preferred_element_type=jnp.float32
    )
    precision_matrix = gram_sum + (members - 1.0) * identity
    forcing = jnp.dot(
        obs_pert,
        obs_weight * (observed - obs_mean),
        precision=lax.Precision.HIGHEST,
        preferred_element_type=jnp.float32,
    )
    norm_scale = jnp.sqrt(jnp.sum(precision_matrix * precision_matrix))
    current = precision_matrix / norm_scale
    root_iter = identity
    for iteration in range(ITERS):
        middle = 1.5 * identity - 0.5 * jnp.dot(
            root_iter, current, precision=lax.Precision.HIGHEST, preferred_element_type=jnp.float32
        )
        current = jnp.dot(
            current, middle, precision=lax.Precision.HIGHEST, preferred_element_type=jnp.float32
        )
        root_iter = jnp.dot(
            middle, root_iter, precision=lax.Precision.HIGHEST, preferred_element_type=jnp.float32
        )
    inv_root = root_iter / jnp.sqrt(norm_scale)
    inner = jnp.dot(
        inv_root, forcing, precision=lax.Precision.HIGHEST, preferred_element_type=jnp.float32
    )
    mean_weights = jnp.dot(
        inv_root, inner, precision=lax.Precision.HIGHEST, preferred_element_type=jnp.float32
    )
    transform = (jnp.sqrt(members - 1.0) * inv_root + mean_weights[:, None]).astype(jnp.bfloat16)
    state_mean = jnp.mean(regional.astype(jnp.float32), axis=0)
    state_pert = (regional.astype(jnp.float32) - state_mean).astype(jnp.bfloat16)
    mixed = lax.dot_general(
        transform, state_pert, (((0,), (0,)), ((), ())), preferred_element_type=jnp.float32
    )
    return (state_mean + mixed).astype(jnp.bfloat16)


def body(states, obs_ens, obs_value, obs_prec, obs_pick, taper):
    position = lax.axis_index("narrow")
    extended = padded(obs_ens, (("wide", 1),), HALO)
    stat_pair = padded(jnp.stack([obs_value, obs_prec]), (("wide", 1),), HALO)
    own_rows = lax.dynamic_index_in_dim(obs_pick, position, 0, keepdims=False)
    gathered = lax.all_gather(extended, "narrow", axis=0, tiled=True)
    picked = jnp.take(gathered, own_rows, axis=1)
    stat_rows = jnp.take(stat_pair, own_rows, axis=1)
    regional = lax.all_to_all(states, "narrow", split_axis=1, concat_axis=0, tiled=True)
    result = analyse(picked.astype(jnp.float32), stat_rows[0], stat_rows[1], taper[0], regional)
    return lax.all_to_all(result, "narrow", split_axis=0, concat_axis=1, tiled=True)


def solution(mesh):
    return jax.shard_map(
        body,
        mesh=mesh,
        in_specs=(
            P("narrow", "wide"),
            P("narrow", "wide"),
            P("wide"),
            P("wide"),
            P("wide", None),
            P(("wide", "narrow"), None),
        ),
        out_specs=P("narrow", "wide"),
        check_vma=False,
    )
```

profile of v0, /device:TPU:1, one launch (start us, length us, event | category | flops | bytes accessed | tf_op | source)
XLA Modules:
  0.0 189.1 jit_solution(3029182865929186891)
XLA Ops:
  6.5 4.6 %copy.29 = bf16[2,16,8,8192]{3,2,0,1:T(8,128)(2,1)} copy(bf16[2,16,8,8192]{3,2,1,0:T(8,128)(2,1)} %bitcast.79) | data formatting | bytes 8388608 | tf_op jit(solution)/shard_map/all_to_all | solution.py:77
  11.2 7.6 %all-to-all-start = ((bf16[16,16,8192]{2,0,1:T(8,128)(2,1)}), bf16[16,16,8192]{2,0,1:T(8,128)(2,1)}, u32[]{:S(2)}, u32[]{:S(2)}) async-start(bf16[16,16,8192]{2,0,1:T(8,128)(2,1)} %bitcast.77), calls=%async_computation | async-start | bytes 8388608 | tf_op jit(solution)/shard_map/all_to_all | solution.py:77
  18.9 1.9 %collective-permute-start = (bf16[16,256]{1,0:T(8,128)(2,1)S(1)}, bf16[16,256]{1,0:T(8,128)(2,1)S(1)}, u32[]{:S(2)}, u32[]{:S(2)}) collective-permute-start(bf16[16,256]{1,0:T(8,128)(2,1)S(1)} %get-tuple-element.10), channel_id=1, source_target_pairs={{0,16},{16,32},{32,48},{48,64},{64,80},{80,96},{96,112},{112,128},... | collective-permute-start | bytes 24584 | tf_op jit(solution)/shard_map/ppermute | solution.py:17
  20.8 5.4 %collective-permute-start.1 = (bf16[16,256]{1,0:T(8,128)(2,1)S(1)}, bf16[16,256]{1,0:T(8,128)(2,1)S(1)}, u32[]{:S(2)}, u32[]{:S(2)}) collective-permute-start(bf16[16,256]{1,0:T(8,128)(2,1)S(1)} %get-tuple-element.11), channel_id=1, source_target_pairs={{16,0},{32,16},{48,32},{64,48},{80,64},{96,80},{112,96},{128,112},... | collective-permute-start | bytes 24584 | tf_op jit(solution)/shard_map/ppermute | solution.py:18
  26.2 39.7 %collective-permute-done = bf16[16,256]{1,0:T(8,128)(2,1)S(1)} collective-permute-done((bf16[16,256]{1,0:T(8,128)(2,1)S(1)}, bf16[16,256]{1,0:T(8,128)(2,1)S(1)}, u32[]{:S(2)}, u32[]{:S(2)}) %collective-permute-start) | collective-permute-done | bytes 8224 | tf_op jit(solution)/shard_map/ppermute | solution.py:17
  65.9 2.8 %collective-permute-done.1 = bf16[16,256]{1,0:T(8,128)(2,1)S(1)} collective-permute-done((bf16[16,256]{1,0:T(8,128)(2,1)S(1)}, bf16[16,256]{1,0:T(8,128)(2,1)S(1)}, u32[]{:S(2)}, u32[]{:S(2)}) %collective-permute-start.1) | collective-permute-done | bytes 8224 | tf_op jit(solution)/shard_map/ppermute | solution.py:18
  68.8 0.7 pad_maximum_fusion
  69.5 1.0 collective-permute-start.2
  70.5 4.9 %collective-permute-start.3 = (f32[2,256]{1,0:T(2,128)S(1)}, f32[2,256]{1,0:T(2,128)S(1)}, u32[]{:S(2)}, u32[]{:S(2)}) collective-permute-start(f32[2,256]{1,0:T(2,128)S(1)} %get-tuple-element.13), channel_id=1, source_target_pairs={{16,0},{32,16},{48,32},{64,48},{80,64},{96,80},{112,96},{128,112},... | collective-permute-start | bytes 6152 | tf_op jit(solution)/shard_map/ppermute | solution.py:18
  75.5 0.8 compare_select_fusion
  76.6 0.7 copy.23
  77.3 2.8 %gather_fusion.1 = f32[1024,2]{1,0:T(8,128)S(1)} fusion(f32[2,4608]{0,1:T(8,128)S(1)} %copy.23, s32[1024]{0:T(1024)S(1)} %broadcast_clamp_fusion), kind=kCustom, calls=%fused_computation.1 | custom fusion | bytes 20480 | tf_op jit(solution)/shard_map/jit(_take)/gather | solution.py:76
  80.3 0.6 fusion.17
  81.0 3.0 %convert_reduce_fusion = f32[8192]{0:T(1024)S(1)} fusion(bf16[16,16,8192]{2,0,1:T(8,128)(2,1)} %all-to-all-done), kind=kLoop, calls=%fused_computation.7 | loop fusion | flops 4186112 | bytes 4227072 | tf_op jit(solution)/shard_map/reduce_sum | solution.py:61
  84.0 5.2 %fusion.1 = bf16[256,8192]{1,0:T(8,128)(2,1)} fusion(f32[8192]{0:T(1024)S(1)} %broadcast_multiply_fusion, bf16[16,16,8192]{2,0,1:T(8,128)(2,1)} %all-to-all-done), kind=kLoop, calls=%fused_computation.5 | loop fusion | flops 6291456 | bytes 8421376 | tf_op jit(solution)/shard_map/convert_element_type | solution.py:62
  89.2 18.3 %all-gather.2.cloned.1.call-done = bf16[256,4608]{1,0:T(8,128)(2,1)} async-done(((bf16[16,4608]{1,0:T(8,128)(2,1)}), bf16[256,4608]{1,0:T(8,128)(2,1)}) %all-gather.2.cloned.1.call-update) | async-done | bytes 2359312 | tf_op jit(solution)/shard_map/all_gather | solution.py:74
  107.5 2.8 %copy.22 = bf16[256,4608]{0,1:T(8,128)(2,1)S(1)} copy(bf16[256,4608]{1,0:T(8,128)(2,1)} %all-gather.2.cloned.1.call-done) | data formatting | bytes 4718592 | tf_op jit(solution)/shard_map/all_gather | solution.py:74
  110.3 4.1 %gather_fusion = bf16[1024,256]{1,0:T(8,128)(2,1)S(1)} fusion(bf16[256,4608]{0,1:T(8,128)(2,1)S(1)} %copy.22, s32[1024]{0:T(1024)S(1)} %broadcast_clamp_fusion), kind=kCustom, calls=%fused_computation | custom fusion | bytes 1052672 | tf_op jit(solution)/shard_map/jit(_take)/gather | solution.py:75
  114.8 1.9 multiply_reduce_fusion
  117.8 0.4 fusion.20
  118.4 0.4 fusion.6
  119.2 0.4 fusion.23
  119.6 0.4 fusion.5
  120.8 0.4 fusion.4
  121.2 0.4 fusion.28
  121.9 0.4 fusion.3
  123.1 0.8 convolution_bitcast_fusion
  123.9 0.4 fusion.2
  124.3 0.4 convolution_divide_fusion
  125.3 1.4 fusion
  126.7 53.1 %all_to_all.32 = bf16[16,16,8192]{2,1,0:T(8,128)(2,1)S(1)} all-to-all(bf16[16,16,8192]{2,1,0:T(8,128)(2,1)S(1)} %bitcast.76), channel_id=1, replica_groups=mesh['wide'=16,'narrow'=16] {'narrow'}, dimensions={0} | all-to-all | bytes 8388608 | tf_op jit(solution)/shard_map/all_to_all | solution.py:79
  179.8 2.5 %copy.27 = bf16[16,2,8,8192]{3,2,0,1:T(8,128)(2,1)} copy(bf16[16,2,8,8192]{3,2,1,0:T(8,128)(2,1)S(1)} %bitcast.78) | data formatting | bytes 8388608 | tf_op jit(solution)/shard_map/all_to_all | solution.py:79
  (35 shorter events, 4.4 us)
Async XLA Ops:
  11.2 7.7 %copy-start.1 = (bf16[16,4096]{1,0:T(8,128)(2,1)S(1)}, bf16[16,4096]{1,0:T(8,128)(2,1)}, u32[]{:S(2)}) copy-start(bf16[16,4096]{1,0:T(8,128)(2,1)} %param.7) | copy-start | bytes 393220
  11.2 58.3 %copy-start.2 = (f32[4096]{0:T(1024)S(1)}, f32[4096]{0:T(1024)}, u32[]{:S(2)}) copy-start(f32[4096]{0:T(1024)} %param.9) | copy-start | bytes 49156
  11.2 58.3 %copy-start.3 = (f32[4096]{0:T(1024)S(1)}, f32[4096]{0:T(1024)}, u32[]{:S(2)}) copy-start(f32[4096]{0:T(1024)} %param.8) | copy-start | bytes 49156
  11.2 65.1 %copy-start.4 = (f32[1,1024]{1,0:T(1,128)S(1)}, f32[1,1024]{1,0:T(1,128)}, u32[]{:S(2)}) copy-start(f32[1,1024]{1,0:T(1,128)} %param.11) | copy-start | bytes 12292
  11.2 69.8 %all-to-all-start = ((bf16[16,16,8192]{2,0,1:T(8,128)(2,1)}), bf16[16,16,8192]{2,0,1:T(8,128)(2,1)}, u32[]{:S(2)}, u32[]{:S(2)}) async-start(bf16[16,16,8192]{2,0,1:T(8,128)(2,1)} %bitcast.77), calls=%async_computation | async-start | bytes 8388608 | tf_op jit(solution)/shard_map/all_to_all | solution.py:77
  18.8 88.7 %all-gather.2.cloned.1.call-start = ((), (), s32[]{:S(2)}) async-start(), calls=%async_computation.2 | async-start | bytes 2506752 | tf_op jit(solution)/shard_map/all_gather | solution.py:74
  18.9 47.0 %collective-permute-start = (bf16[16,256]{1,0:T(8,128)(2,1)S(1)}, bf16[16,256]{1,0:T(8,128)(2,1)S(1)}, u32[]{:S(2)}, u32[]{:S(2)}) collective-permute-start(bf16[16,256]{1,0:T(8,128)(2,1)S(1)} %get-tuple-element.10), channel_id=1, source_target_pairs={{0,16},{16,32},{32,48},{48,64},{64,80},{80,96},{96,112},{112,128},... | collective-permute-start | bytes 24584 | tf_op jit(solution)/shard_map/ppermute | solution.py:17
  20.8 47.9 %collective-permute-start.1 = (bf16[16,256]{1,0:T(8,128)(2,1)S(1)}, bf16[16,256]{1,0:T(8,128)(2,1)S(1)}, u32[]{:S(2)}, u32[]{:S(2)}) collective-permute-start(bf16[16,256]{1,0:T(8,128)(2,1)S(1)} %get-tuple-element.11), channel_id=1, source_target_pairs={{16,0},{32,16},{48,32},{64,48},{80,64},{96,80},{112,96},{128,112},... | collective-permute-start | bytes 24584 | tf_op jit(solution)/shard_map/ppermute | solution.py:18
  69.5 7.0 %collective-permute-start.2 = (f32[2,256]{1,0:T(2,128)S(1)}, f32[2,256]{1,0:T(2,128)S(1)}, u32[]{:S(2)}, u32[]{:S(2)}) collective-permute-start(f32[2,256]{1,0:T(2,128)S(1)} %get-tuple-element.12), channel_id=1, source_target_pairs={{0,16},{16,32},{32,48},{48,64},{64,80},{80,96},{96,112},{112,128},... | collective-permute-start | bytes 6152 | tf_op jit(solution)/shard_map/ppermute | solution.py:17
  70.5 6.0 %collective-permute-start.3 = (f32[2,256]{1,0:T(2,128)S(1)}, f32[2,256]{1,0:T(2,128)S(1)}, u32[]{:S(2)}, u32[]{:S(2)}) collective-permute-start(f32[2,256]{1,0:T(2,128)S(1)} %get-tuple-element.13), channel_id=1, source_target_pairs={{16,0},{32,16},{48,32},{64,48},{80,64},{96,80},{112,96},{128,112},... | collective-permute-start | bytes 6152 | tf_op jit(solution)/shard_map/ppermute | solution.py:18
  120.8 4.5 %copy-start = (bf16[256,8192]{1,0:T(8,128)(2,1)S(1)}, bf16[256,8192]{1,0:T(8,128)(2,1)}, u32[]{:S(2)}) copy-start(bf16[256,8192]{1,0:T(8,128)(2,1)} %fusion.1) | copy-start | bytes 12582916
Sparse Core Ops, SparseCore 0:
  69.6 37.8 all-gather.1
where the time goes:
time: 189 us
  waiting for transfers between devices  60.9 us (32%)
  blocking collectives  53.1 us (28%)
  starting transfers between devices  21 us (11%)
  local copies, waits for them, and re-layouts  17.8 us (9%)
  between operations  14.4 us (8%)
  matrix products  11 us (6%)
  other arithmetic  10.9 us (6%)
    all_to_all x1, blocking collectives, body(): lax.all_to_all(result, 'narrow', split_axis=0, concat_axis=1, tiled=True)  53.1 us
    ppermute x2, waiting for transfers between devices, padded(): before = lax.ppermute(last, axis, up)  39.7 us
    all_gather x1, waiting for transfers between devices, body(): gathered = lax.all_gather(extended, 'narrow', axis=0, tiled=True)  18.3 us
    ppermute x2, starting transfers between devices, padded(): after = lax.ppermute(leading, axis, down)  10.3 us
    all_to_all x1, starting transfers between devices, body(): lax.all_to_all(states, 'narrow', split_axis=1, concat_axis=0, tiled=True)  7.64 us
    convert_element_type x1, other arithmetic, analyse(): (regional.astype(jnp.float32) - state_mean).astype(jnp.bfloat16)  5.21 us
    all_to_all x1, local copies, waits for them, and re-layouts, body(): lax.all_to_all(states, 'narrow', split_axis=1, concat_axis=0, tiled=True)  4.64 us
    gather x1, local copies, waits for them, and re-layouts, body(): picked = jnp.take(gathered, own_rows, axis=1)  4.12 us
  transfers between devices with their start and end apart: 6, of which 3 were waited for; matrix products, arithmetic and copies ran while one was open for 8% of the time, Pallas kernels for 0%

commit v1 on v0

v1 whole, which is shorter than its diff:
```python
import functools
import math

import jax
import jax.numpy as jnp
from jax import lax
from jax.experimental import pallas as pl
from jax.experimental.pallas import tpu as pltpu
from jax.sharding import PartitionSpec as P

MEMBERS = 256
OWN = 16
CELLS = 8192
OBS_W = 4096
HALO = 256
WIN = OBS_W + 2 * HALO
NPICK = 1024
ITERS = 6
N_WIDE = 16
N_NARROW = 16
LANES = 128
WIN_ROWS = WIN // LANES
CHUNKS = 8
CHUNK = CELLS // CHUNKS
TILE = 256
MESH = pl.DeviceIdType.MESH
HIGH = lax.Precision.HIGHEST
NT = (((1,), (1,)), ((), ()))

PEERS = [
    (dy, dx, dc)
    for dy in (2, 1, 3, 0)
    for dx in (1, 0)
    for dc in (1, 0)
    if (dy, dx, dc) != (0, 0, 0)
]


def kernel(states, obs, value, prec, pick, taper, out,
           inbuf, outbuf, win, vtiles, ptiles, vwin, pwin, tapwin, gram, facc, trans,
           in_send, in_recv, out_send, out_recv, loc_sem, halo_send, halo_recv, obs_send, obs_recv):
    w = lax.axis_index("wide")
    n = lax.axis_index("narrow")
    y, x, c = n // 4, (n // 2) % 2, n % 2

    def at(dy, dx, dc):
        yy, xx, cc = (y + dy) % 4, (x + dx) % 2, (c + dc) % 2
        return 4 * yy + 2 * xx + cc, 4 * yy + 2 * cc + xx

    peers = [at(*d) for d in PEERS]
    before, after = (w + N_WIDE - 1) % N_WIDE, (w + 1) % N_WIDE
    me = 4 * y + 2 * c + x

    def rows(slot, count=1):
        return pl.ds(pl.multiple_of(slot * OWN, OWN), count * OWN)

    barrier = pltpu.get_barrier_semaphore()
    for index, _ in peers:
        pl.semaphore_signal(barrier, inc=1, device_id=(w, index), device_id_type=MESH)
    for band in (before, after):
        pl.semaphore_signal(barrier, inc=1, device_id=(band, n), device_id_type=MESH)
    pl.semaphore_wait(barrier, len(PEERS) + 2)

    def remote(src, dst, send, recv, device):
        return pltpu.make_async_remote_copy(
            src_ref=src, dst_ref=dst, send_sem=send, recv_sem=recv, device_id=device, device_id_type=MESH
        )

    mine = rows(me)
    halos = [
        remote(obs.at[:, pl.ds(OBS_W - HALO, HALO)], win.at[mine, pl.ds(0, HALO)],
               halo_send.at[0], halo_recv.at[0], (after, n)),
        remote(obs.at[:, pl.ds(0, HALO)], win.at[mine, pl.ds(HALO + OBS_W, HALO)],
               halo_send.at[1], halo_recv.at[1], (before, n)),
        remote(value.at[pl.ds(24, 8)], vtiles.at[0], halo_send.at[2], halo_recv.at[2], (after, n)),
        remote(value.at[pl.ds(0, 8)], vtiles.at[1], halo_send.at[3], halo_recv.at[3], (before, n)),
        remote(prec.at[pl.ds(24, 8)], ptiles.at[0], halo_send.at[4], halo_recv.at[4], (after, n)),
        remote(prec.at[pl.ds(0, 8)], ptiles.at[1], halo_send.at[5], halo_recv.at[5], (before, n)),
    ]
    for copy in halos:
        copy.start()
    own_obs = pltpu.make_async_copy(obs, win.at[mine, pl.ds(HALO, OBS_W)], loc_sem.at[0])
    own_obs.start()
    own_states = pltpu.make_async_copy(
        states.at[:, pl.ds(pl.multiple_of(n * CELLS, CELLS), CELLS)], inbuf.at[mine], loc_sem.at[1]
    )
    own_states.start()

    def send_states(chunk):
        for index, _ in peers:
            start = pl.multiple_of(index * CELLS + chunk * CHUNK, CHUNK)
            remote(states.at[:, pl.ds(start, CHUNK)],
                   inbuf.at[mine, pl.ds(pl.multiple_of(chunk * CHUNK, CHUNK), CHUNK)],
                   in_send.at[chunk], in_recv.at[chunk], (w, index)).start()

    send_states(0)

    def move(slot, count, index, sem):
        block = win.at[rows(slot, count)]
        return remote(block, block, obs_send.at[sem], obs_recv.at[sem], (w, index))

    other_core, _ = at(0, 0, 1)
    x_peer, _ = at(0, 1, 0)
    up, _ = at(1, 0, 0)
    down, _ = at(3, 0, 0)

    def pair(dy):
        return 4 * ((y + dy) % 4) + 2 * c

    own_obs.wait()
    halos[0].wait_recv()
    halos[1].wait_recv()
    to_x = move(me, 1, x_peer, 0)
    to_x.start()
    send_states(1)
    to_x.wait_recv()
    to_up = move(pair(0), 2, up, 1)
    to_down = move(pair(0), 2, down, 2)
    to_core0 = move(pair(0), 2, other_core, 3)
    to_up.start()
    to_down.start()
    to_core0.start()
    send_states(2)
    to_up.wait_recv()
    on_up = move(pair(3), 1, up, 4)
    on_up.start()
    to_core1 = move(pair(3), 2, other_core, 5)
    to_core1.start()
    to_down.wait_recv()
    on_down = move(pair(1) + 1, 1, down, 6)
    on_down.start()
    to_core2 = move(pair(1), 2, other_core, 7)
    to_core2.start()
    send_states(3)
    on_up.wait_recv()
    on_down.wait_recv()
    to_core3 = move(pair(2), 2, other_core, 8)
    to_core3.start()

    @pl.loop(4, CHUNKS)
    def _(chunk):
        send_states(chunk)

    for copy in halos[2:]:
        copy.wait_recv()
    vwin[0:2] = vtiles[0, 6:8]
    vwin[2:34] = value[...]
    vwin[34:36] = vtiles[1, 0:2]
    pwin[0:2] = ptiles[0, 6:8]
    pwin[2:34] = prec[...]
    pwin[34:36] = ptiles[1, 0:2]
    own_pick = pick[pl.ds(n, 1), :]
    coarse = lax.broadcasted_iota(jnp.int32, (40, NPICK), 0) == (own_pick >> 7)
    fine = lax.broadcasted_iota(jnp.int32, (LANES, NPICK), 0) == (own_pick & 127)
    tapwin[...] = lax.dot_general(
        jnp.where(coarse, taper[...], 0.0), fine.astype(jnp.float32), NT,
        precision=HIGH, preferred_element_type=jnp.float32,
    )
    gram[...] = jnp.zeros_like(gram)
    facc[...] = jnp.zeros_like(facc)
    for copy in (to_core0, to_core1, to_core2, to_core3):
        copy.wait_recv()

    @pl.loop(0, WIN // TILE)
    def _(tile):
        columns = pl.ds(pl.multiple_of(tile * TILE, TILE), TILE)

        def flat(ref):
            return jnp.concatenate([ref[pl.ds(2 * tile, 1), :], ref[pl.ds(2 * tile + 1, 1), :]], axis=1)

        ensemble = win[:, columns].astype(jnp.float32)
        mean = jnp.sum(ensemble, axis=0, keepdims=True) * (1.0 / MEMBERS)
        pert = ensemble - mean
        weight = flat(pwin) * flat(tapwin)
        scaled = (pert * jnp.sqrt(weight)).astype(jnp.bfloat16)
        gram[...] += lax.dot_general(scaled, scaled, NT, preferred_element_type=jnp.float32)
        force = pert * (weight * (flat(vwin) - mean))
        facc[...] += force[:, :LANES] + force[:, LANES:]

    identity = (
        lax.broadcasted_iota(jnp.int32, (MEMBERS, MEMBERS), 0)
        == lax.broadcasted_iota(jnp.int32, (MEMBERS, MEMBERS), 1)
    ).astype(jnp.float32)

    def dot(a, b):
        return jnp.dot(a, b, precision=HIGH, preferred_element_type=jnp.float32)

    matrix = gram[...] + (MEMBERS - 1.0) * identity
    scale = jnp.sqrt(jnp.sum(jnp.sum(matrix * matrix, axis=0, keepdims=True), axis=1, keepdims=True))
    gram[...] = matrix / scale
    trans[...] = identity

    @pl.loop(0, ITERS)
    def _(_):
        current, root = gram[...], trans[...]
        middle = 1.5 * identity - 0.5 * dot(root, current)
        gram[...] = dot(current, middle)
        trans[...] = dot(middle, root)

    inv_root = trans[...] / jnp.sqrt(scale)
    force = lax.dot_general(
        jnp.ones((8, LANES), jnp.float32), facc[...], NT, precision=HIGH, preferred_element_type=jnp.float32
    )
    inner = lax.dot_general(force, inv_root, NT, precision=HIGH, preferred_element_type=jnp.float32)
    weights = lax.dot_general(inner, inv_root, NT, precision=HIGH, preferred_element_type=jnp.float32)
    transform = (math.sqrt(MEMBERS - 1.0) * inv_root + weights[0:1]).astype(jnp.bfloat16)
    trans[...] = transform.astype(jnp.float32)
    own_states.wait()

    @pl.loop(0, CHUNKS)
    def _(chunk):
        columns = pl.ds(pl.multiple_of(chunk * CHUNK, CHUNK), CHUNK)
        arrived = inbuf.at[pl.ds(0, MEMBERS - OWN), columns]
        pltpu.make_async_copy(arrived, arrived, in_recv.at[chunk]).wait()
        mixer = trans[...].astype(jnp.bfloat16)

        @pl.loop(0, CHUNK // TILE)
        def _(tile):
            part = pl.ds(pl.multiple_of(chunk * CHUNK + tile * TILE, TILE), TILE)
            entries = inbuf[:, part].astype(jnp.float32)
            mean = jnp.sum(entries, axis=0, keepdims=True) * (1.0 / MEMBERS)
            pert = (entries - mean).astype(jnp.bfloat16)
            mixed = jnp.dot(mixer, pert, preferred_element_type=jnp.float32)
            outbuf[:, part] = (mean + mixed).astype(jnp.bfloat16)

        target = pl.ds(pl.multiple_of(n * CELLS + chunk * CHUNK, CHUNK), CHUNK)
        for index, slot in peers:
            remote(outbuf.at[rows(slot), columns], out.at[:, target],
                   out_send.at[chunk], out_recv.at[chunk], (w, index)).start()

    own_out = pltpu.make_async_copy(
        outbuf.at[mine], out.at[:, pl.ds(pl.multiple_of(n * CELLS, CELLS), CELLS)], loc_sem.at[2]
    )
    own_out.start()
    for copy in halos:
        copy.wait_send()
    for copy in (to_x, to_up, to_down, on_up, on_down, to_core0, to_core1, to_core2, to_core3):
        copy.wait_send()

    @pl.loop(0, CHUNKS)
    def _(chunk):
        columns = pl.ds(pl.multiple_of(chunk * CHUNK, CHUNK), CHUNK)
        most = outbuf.at[pl.ds(0, MEMBERS - OWN), columns]
        pltpu.make_async_copy(most, most, in_send.at[chunk]).wait()
        pltpu.make_async_copy(most, most, out_send.at[chunk]).wait()
        pltpu.make_async_copy(most, most, out_recv.at[chunk]).wait()

    own_out.wait()


def body(states, obs_ens, obs_value, obs_prec, obs_pick, taper):
    vmem, hbm = (pl.BlockSpec(memory_space=pltpu.VMEM), pl.BlockSpec(memory_space=pl.ANY))
    dma = pltpu.SemaphoreType.DMA
    return pl.pallas_call(
        kernel,
        out_shape=jax.ShapeDtypeStruct(states.shape, jnp.bfloat16),
        in_specs=[hbm, vmem, vmem, vmem, vmem, vmem],
        out_specs=hbm,
        scratch_shapes=[
            pltpu.VMEM((MEMBERS, CELLS), jnp.bfloat16),
            pltpu.VMEM((MEMBERS, CELLS), jnp.bfloat16),
            pltpu.VMEM((MEMBERS, WIN), jnp.bfloat16),
            pltpu.VMEM((2, 8, LANES), jnp.float32),
            pltpu.VMEM((2, 8, LANES), jnp.float32),
            pltpu.VMEM((40, LANES), jnp.float32),
            pltpu.VMEM((40, LANES), jnp.float32),
            pltpu.VMEM((40, LANES), jnp.float32),
            pltpu.VMEM((MEMBERS, MEMBERS), jnp.float32),
            pltpu.VMEM((MEMBERS, LANES), jnp.float32),
            pltpu.VMEM((MEMBERS, MEMBERS), jnp.float32),
            dma((CHUNKS,)),
            dma((CHUNKS,)),
            dma((CHUNKS,)),
            dma((CHUNKS,)),
            dma((3,)),
            dma((6,)),
            dma((6,)),
            dma((9,)),
            dma((9,)),
        ],
        compiler_params=pltpu.CompilerParams(
            collective_id=0, has_side_effects=True, vmem_limit_bytes=40 << 20
        ),
        name="analysis",
    )(states, obs_ens, obs_value.reshape(OBS_W // LANES, LANES), obs_prec.reshape(OBS_W // LANES, LANES), obs_pick, taper)


def solution(mesh):
    return jax.shard_map(
        body,
        mesh=mesh,
        in_specs=(
            P("narrow", "wide"),
            P("narrow", "wide"),
            P("wide"),
            P("wide"),
            P("wide", None),
            P(("wide", "narrow"), None),
        ),
        out_specs=P("narrow", "wide"),
        check_vma=False,
    )
```

time: 189 us -> 124 us (0.66)
  Pallas kernels: 0 us -> 116 us
  waiting for transfers between devices: 60.9 us -> 0 us
  blocking collectives: 53.1 us -> 0 us
  starting transfers between devices: 21 us -> 0 us
  between operations: 14.4 us -> 0.02 us
  matrix products: 11 us -> 0 us
  other arithmetic: 10.9 us -> 0 us
  local copies, waits for them, and re-layouts: 17.8 us -> 8.07 us
    pallas_call x0 -> x1, Pallas kernels: none -> 116 us  [body(): pl.pallas_call(kernel, out_shape=jax.ShapeDtypeStruct(states.shape, jnp.b...]
    all_to_all x1 -> x0, blocking collectives: 53.1 us -> none  [body(): lax.all_to_all(result, 'narrow', split_axis=0, concat_axis=1, tiled=True)]
    ppermute x4 -> x0, waiting for transfers between devices: 42.5 us -> none  [the longest x2 39.7 us: padded(): before = lax.ppermute(last, axis, up)]
    all_gather x1 -> x0, waiting for transfers between devices: 18.3 us -> none  [body(): gathered = lax.all_gather(extended, 'narrow', axis=0, tiled=True)]
    ppermute x4 -> x0, starting transfers between devices: 13.3 us -> none  [the longest x2 10.3 us: padded(): after = lax.ppermute(leading, axis, down)]
    dot_general x22 -> x0, matrix products: 11 us -> none  [the longest x6 2.22 us: analyse(): jnp.dot(root_iter, current, precision=lax.Precision.HIGHEST, preferred_el...]
    unnamed x11 -> x13, local copies, waits for them, and re-layouts: 0.24 us -> 8.07 us
    all_to_all x1 -> x0, starting transfers between devices: 7.64 us -> none  [body(): lax.all_to_all(states, 'narrow', split_axis=1, concat_axis=0, tiled=True)]
  transfers between devices with their start and end apart: 6 -> 0, of which waited for: 3 -> 0; matrix products, arithmetic and copies ran while one was open for 8% -> 0% of each run, Pallas kernels for 0% -> 0%
where the time goes in v1:
time: 124 us
  Pallas kernels  116 us (94%)
  local copies, waits for them, and re-layouts  8.07 us (7%)
    pallas_call x1, Pallas kernels, body(): pl.pallas_call(kernel, out_shape=jax.ShapeDtypeStruct(states.shape, jnp.b...  116 us
    unnamed x13, local copies, waits for them, and re-layouts  8.07 us

profile of v1, /device:TPU:1, one launch (start us, length us, event | category | flops | bytes accessed | tf_op | source)
XLA Modules:
  0.0 123.9 jit_solution(538309473353895517)
XLA Ops:
  0.0 0.0 copy-start
  0.0 2.2 %copy-done = bf16[16,131072]{1,0:T(8,128)(2,1)S(1)} copy-done((bf16[16,131072]{1,0:T(8,128)(2,1)S(1)}, bf16[16,131072]{1,0:T(8,128)(2,1)}, u32[]{:S(2)}) %copy-start) | copy-done | bytes 4194328
  2.2 0.0 copy-start.1
  2.2 0.9 copy-done.1
  3.1 0.0 copy-start.2
  3.1 0.8 copy-done.2
  3.9 0.0 copy-start.3
  3.9 0.7 copy-done.3
  4.7 0.0 copy-start.4
  4.7 0.7 copy-done.4
  5.4 0.0 copy-start.5
  5.4 0.7 copy-done.5
  6.1 115.9 %analysis.1 = bf16[16,131072]{1,0:T(8,128)(2,1)S(1)} custom-call(bf16[16,131072]{1,0:T(8,128)(2,1)S(1)} %copy-done, bf16[16,4096]{1,0:T(8,128)(2,1)S(1)} %copy-done.1, f32[32,128]{1,0:T(8,128)S(1)} %bitcast.2, f32[32,128]{1,0:T(8,128)S(1)} %bitcast.3, s32[16,1024]{1,0:T(8,128)S(1)} %copy-done.2, f32[1,1024]{1,0:T(1,128)S(1)} %copy-done.5), custom_call_target="tpu_custom_call" | custom-call | tf_op jit(solution)/shard_map/analysis/pallas_call | solution.py:254
  121.9 2.0 %copy.8 = bf16[16,131072]{1,0:T(8,128)(2,1)} copy(bf16[16,131072]{1,0:T(8,128)(2,1)S(1)} %analysis.1) | data formatting | bytes 8388608
Async XLA Ops:
  0.0 2.2 %copy-start = (bf16[16,131072]{1,0:T(8,128)(2,1)S(1)}, bf16[16,131072]{1,0:T(8,128)(2,1)}, u32[]{:S(2)}) copy-start(bf16[16,131072]{1,0:T(8,128)(2,1)} %states.1) | copy-start | bytes 12582916
  2.2 0.9 copy-start.1
  3.1 0.8 copy-start.2
  3.9 0.7 copy-start.3
  4.7 0.7 copy-start.4
  5.4 0.7 copy-start.5

commit v2 on v1

--- a/solution.py
+++ b/solution.py
@@ -37,7 +37,7 @@
 
 
 def kernel(states, obs, value, prec, pick, taper, out,
-           inbuf, outbuf, win, vtiles, ptiles, vwin, pwin, tapwin, gram, facc, trans,
+           inbuf, outbuf, win, vwin, pwin, picked, tap, tapwin, gram, facc, trans,
            in_send, in_recv, out_send, out_recv, loc_sem, halo_send, halo_recv, obs_send, obs_recv):
     w = lax.axis_index("wide")
     n = lax.axis_index("narrow")
@@ -57,9 +57,8 @@
     barrier = pltpu.get_barrier_semaphore()
     for index, _ in peers:
         pl.semaphore_signal(barrier, inc=1, device_id=(w, index), device_id_type=MESH)
-    for band in (before, after):
-        pl.semaphore_signal(barrier, inc=1, device_id=(band, n), device_id_type=MESH)
-    pl.semaphore_wait(barrier, len(PEERS) + 2)
+    pl.semaphore_signal(barrier, inc=1, device_id=(before, n), device_id_type=MESH)
+    pl.semaphore_wait(barrier, len(PEERS) + 1)
 
     def remote(src, dst, send, recv, device):
         return pltpu.make_async_remote_copy(
@@ -72,12 +71,12 @@
                halo_send.at[0], halo_recv.at[0], (after, n)),
         remote(obs.at[:, pl.ds(0, HALO)], win.at[mine, pl.ds(HALO + OBS_W, HALO)],
                halo_send.at[1], halo_recv.at[1], (before, n)),
-        remote(value.at[pl.ds(24, 8)], vtiles.at[0], halo_send.at[2], halo_recv.at[2], (after, n)),
-        remote(value.at[pl.ds(0, 8)], vtiles.at[1], halo_send.at[3], halo_recv.at[3], (before, n)),
-        remote(prec.at[pl.ds(24, 8)], ptiles.at[0], halo_send.at[4], halo_recv.at[4], (after, n)),
-        remote(prec.at[pl.ds(0, 8)], ptiles.at[1], halo_send.at[5], halo_recv.at[5], (before, n)),
+        remote(value.at[pl.ds(24, 8)], vwin.at[pl.ds(0, 8)], halo_send.at[2], halo_recv.at[2], (after, n)),
+        remote(value.at[pl.ds(0, 8)], vwin.at[pl.ds(40, 8)], halo_send.at[3], halo_recv.at[3], (before, n)),
+        remote(prec.at[pl.ds(24, 8)], pwin.at[pl.ds(0, 8)], halo_send.at[4], halo_recv.at[4], (after, n)),
+        remote(prec.at[pl.ds(0, 8)], pwin.at[pl.ds(40, 8)], halo_send.at[5], halo_recv.at[5], (before, n)),
     ]
-    for copy in halos:
+    for copy in halos[0::2]:
         copy.start()
     own_obs = pltpu.make_async_copy(obs, win.at[mine, pl.ds(HALO, OBS_W)], loc_sem.at[0])
     own_obs.start()
@@ -85,6 +84,14 @@
         states.at[:, pl.ds(pl.multiple_of(n * CELLS, CELLS), CELLS)], inbuf.at[mine], loc_sem.at[1]
     )
     own_states.start()
+    smalls = [
+        pltpu.make_async_copy(value, vwin.at[pl.ds(8, 32)], loc_sem.at[3]),
+        pltpu.make_async_copy(prec, pwin.at[pl.ds(8, 32)], loc_sem.at[4]),
+        pltpu.make_async_copy(pick.at[pl.ds(pl.multiple_of(n // 8 * 8, 8), 8)], picked, loc_sem.at[5]),
+        pltpu.make_async_copy(taper, tap, loc_sem.at[6]),
+    ]
+    for copy in smalls:
+        copy.start()
 
     def send_states(chunk):
         for index, _ in peers:
@@ -109,6 +116,8 @@
 
     own_obs.wait()
     halos[0].wait_recv()
+    for copy in halos[1::2]:
+        copy.start()
     halos[1].wait_recv()
     to_x = move(me, 1, x_peer, 0)
     to_x.start()
@@ -141,23 +150,19 @@
     def _(chunk):
         send_states(chunk)
 
-    for copy in halos[2:]:
-        copy.wait_recv()
-    vwin[0:2] = vtiles[0, 6:8]
-    vwin[2:34] = value[...]
-    vwin[34:36] = vtiles[1, 0:2]
-    pwin[0:2] = ptiles[0, 6:8]
-    pwin[2:34] = prec[...]
-    pwin[34:36] = ptiles[1, 0:2]
-    own_pick = pick[pl.ds(n, 1), :]
+    for copy in smalls:
+        copy.wait()
+    own_pick = picked[pl.ds(n % 8, 1), :]
     coarse = lax.broadcasted_iota(jnp.int32, (40, NPICK), 0) == (own_pick >> 7)
     fine = lax.broadcasted_iota(jnp.int32, (LANES, NPICK), 0) == (own_pick & 127)
     tapwin[...] = lax.dot_general(
-        jnp.where(coarse, taper[...], 0.0), fine.astype(jnp.float32), NT,
+        jnp.where(coarse, tap[...], 0.0), fine.astype(jnp.float32), NT,
         precision=HIGH, preferred_element_type=jnp.float32,
     )
     gram[...] = jnp.zeros_like(gram)
     facc[...] = jnp.zeros_like(facc)
+    for copy in halos[2:]:
+        copy.wait_recv()
     for copy in (to_core0, to_core1, to_core2, to_core3):
         copy.wait_recv()
 
@@ -165,16 +170,17 @@
     def _(tile):
         columns = pl.ds(pl.multiple_of(tile * TILE, TILE), TILE)
 
-        def flat(ref):
-            return jnp.concatenate([ref[pl.ds(2 * tile, 1), :], ref[pl.ds(2 * tile + 1, 1), :]], axis=1)
+        def flat(ref, first):
+            row = first + 2 * tile
+            return jnp.concatenate([ref[pl.ds(row, 1), :], ref[pl.ds(row + 1, 1), :]], axis=1)
 
         ensemble = win[:, columns].astype(jnp.float32)
         mean = jnp.sum(ensemble, axis=0, keepdims=True) * (1.0 / MEMBERS)
         pert = ensemble - mean
-        weight = flat(pwin) * flat(tapwin)
+        weight = flat(pwin, 6) * flat(tapwin, 0)
         scaled = (pert * jnp.sqrt(weight)).astype(jnp.bfloat16)
         gram[...] += lax.dot_general(scaled, scaled, NT, preferred_element_type=jnp.float32)
-        force = pert * (weight * (flat(vwin) - mean))
+        force = pert * (weight * (flat(vwin, 6) - mean))
         facc[...] += force[:, :LANES] + force[:, LANES:]
 
     identity = (
@@ -249,21 +255,21 @@
 
 
 def body(states, obs_ens, obs_value, obs_prec, obs_pick, taper):
-    vmem, hbm = (pl.BlockSpec(memory_space=pltpu.VMEM), pl.BlockSpec(memory_space=pl.ANY))
+    hbm, anywhere = (pl.BlockSpec(memory_space=pltpu.HBM), pl.BlockSpec(memory_space=pl.ANY))
     dma = pltpu.SemaphoreType.DMA
     return pl.pallas_call(
         kernel,
         out_shape=jax.ShapeDtypeStruct(states.shape, jnp.bfloat16),
-        in_specs=[hbm, vmem, vmem, vmem, vmem, vmem],
-        out_specs=hbm,
+        in_specs=[hbm] * 6,
+        out_specs=anywhere,
         scratch_shapes=[
             pltpu.VMEM((MEMBERS, CELLS), jnp.bfloat16),
             pltpu.VMEM((MEMBERS, CELLS), jnp.bfloat16),
             pltpu.VMEM((MEMBERS, WIN), jnp.bfloat16),
-            pltpu.VMEM((2, 8, LANES), jnp.float32),
-            pltpu.VMEM((2, 8, LANES), jnp.float32),
-            pltpu.VMEM((40, LANES), jnp.float32),
-            pltpu.VMEM((40, LANES), jnp.float32),
+            pltpu.VMEM((48, LANES), jnp.float32),
+            pltpu.VMEM((48, LANES), jnp.float32),
+            pltpu.VMEM((8, NPICK), jnp.int32),
+            pltpu.VMEM((1, NPICK), jnp.float32),
             pltpu.VMEM((40, LANES), jnp.float32),
             pltpu.VMEM((MEMBERS, MEMBERS), jnp.float32),
             pltpu.VMEM((MEMBERS, LANES), jnp.float32),
@@ -272,14 +278,14 @@
             dma((CHUNKS,)),
             dma((CHUNKS,)),
             dma((CHUNKS,)),
-            dma((3,)),
+            dma((7,)),
             dma((6,)),
             dma((6,)),
             dma((9,)),
             dma((9,)),
         ],
         compiler_params=pltpu.CompilerParams(
-            collective_id=0, has_side_effects=True, vmem_limit_bytes=40 << 20
+            collective_id=0, has_side_effects=True, vmem_limit_bytes=48 << 20
         ),
         name="analysis",
     )(states, obs_ens, obs_value.reshape(OBS_W // LANES, LANES), obs_prec.reshape(OBS_W // LANES, LANES), obs_pick, taper)

time: 124 us -> 121 us (0.976)
  the two profiles are of different devices: /device:TPU:1 before, /device:TPU:103 now
where the time goes in v2:
time: 121 us
  Pallas kernels  115 us (95%)
  local copies, waits for them, and re-layouts  5.88 us (5%)
    pallas_call x1, Pallas kernels, body(): pl.pallas_call(kernel, out_shape=jax.ShapeDtypeStruct(states.shape, jnp.b...  115 us
    unnamed x11, local copies, waits for them, and re-layouts  5.88 us

profile of v2, /device:TPU:103, one launch (start us, length us, event | category | flops | bytes accessed | tf_op | source)
XLA Modules:
  0.0 120.7 jit_solution(12027106717169216497)
XLA Ops:
  0.0 0.0 copy-start
  0.0 0.9 copy-done
  0.9 0.0 copy-start.1
  0.9 0.8 copy-done.1
  1.7 0.0 copy-start.2
  1.7 0.7 copy-done.2
  2.5 0.0 copy-start.3
  2.5 0.7 copy-done.3
  3.2 0.0 copy-start.4
  3.2 0.7 copy-done.4
  3.9 114.8 %analysis.1 = bf16[16,131072]{1,0:T(8,128)(2,1)S(1)} custom-call(bf16[16,131072]{1,0:T(8,128)(2,1)} %states.1, bf16[16,4096]{1,0:T(8,128)(2,1)S(1)} %copy-done, f32[32,128]{1,0:T(8,128)S(1)} %bitcast.2, f32[32,128]{1,0:T(8,128)S(1)} %bitcast.3, s32[16,1024]{1,0:T(8,128)S(1)} %copy-done.1, f32[1,1024]{1,0:T(1,128)S(1)} %copy-done.4), custom_call_target="tpu_custom_call" | custom-call | tf_op jit(solution)/shard_map/analysis/pallas_call | solution.py:260
  118.6 2.0 %copy.8 = bf16[16,131072]{1,0:T(8,128)(2,1)} copy(bf16[16,131072]{1,0:T(8,128)(2,1)S(1)} %analysis.1) | data formatting | bytes 8388608
Async XLA Ops:
  0.0 0.9 copy-start
  0.9 0.8 copy-start.1
  1.7 0.7 copy-start.2
  2.5 0.7 copy-start.3
  3.2 0.7 copy-start.4

commit v3 on v2

--- a/solution.py
+++ b/solution.py
@@ -28,16 +28,13 @@
 NT = (((1,), (1,)), ((), ()))
 
 PEERS = [
-    (dy, dx, dc)
-    for dy in (2, 1, 3, 0)
-    for dx in (1, 0)
-    for dc in (1, 0)
-    if (dy, dx, dc) != (0, 0, 0)
+    (1, 0, 0), (0, 1, 0), (3, 0, 1), (2, 1, 1), (1, 0, 1), (0, 1, 1), (3, 0, 0), (2, 0, 0),
+    (1, 1, 0), (2, 0, 1), (3, 1, 1), (1, 1, 1), (2, 1, 0), (3, 1, 0), (0, 0, 1),
 ]
 
 
-def kernel(states, obs, value, prec, pick, taper, out,
-           inbuf, outbuf, win, vwin, pwin, picked, tap, tapwin, gram, facc, trans,
+def kernel(states, obs, small, out,
+           inbuf, outbuf, win, vwin, pwin, picks, tapwin, gram, facc, trans,
            in_send, in_recv, out_send, out_recv, loc_sem, halo_send, halo_recv, obs_send, obs_recv):
     w = lax.axis_index("wide")
     n = lax.axis_index("narrow")
@@ -71,10 +68,10 @@
                halo_send.at[0], halo_recv.at[0], (after, n)),
         remote(obs.at[:, pl.ds(0, HALO)], win.at[mine, pl.ds(HALO + OBS_W, HALO)],
                halo_send.at[1], halo_recv.at[1], (before, n)),
-        remote(value.at[pl.ds(24, 8)], vwin.at[pl.ds(0, 8)], halo_send.at[2], halo_recv.at[2], (after, n)),
-        remote(value.at[pl.ds(0, 8)], vwin.at[pl.ds(40, 8)], halo_send.at[3], halo_recv.at[3], (before, n)),
-        remote(prec.at[pl.ds(24, 8)], pwin.at[pl.ds(0, 8)], halo_send.at[4], halo_recv.at[4], (after, n)),
-        remote(prec.at[pl.ds(0, 8)], pwin.at[pl.ds(40, 8)], halo_send.at[5], halo_recv.at[5], (before, n)),
+        remote(small.at[pl.ds(24, 8)], vwin.at[pl.ds(0, 8)], halo_send.at[2], halo_recv.at[2], (after, n)),
+        remote(small.at[pl.ds(0, 8)], vwin.at[pl.ds(40, 8)], halo_send.at[3], halo_recv.at[3], (before, n)),
+        remote(small.at[pl.ds(56, 8)], pwin.at[pl.ds(0, 8)], halo_send.at[4], halo_recv.at[4], (after, n)),
+        remote(small.at[pl.ds(32, 8)], pwin.at[pl.ds(40, 8)], halo_send.at[5], halo_recv.at[5], (before, n)),
     ]
     for copy in halos[0::2]:
         copy.start()
@@ -85,10 +82,9 @@
     )
     own_states.start()
     smalls = [
-        pltpu.make_async_copy(value, vwin.at[pl.ds(8, 32)], loc_sem.at[3]),
-        pltpu.make_async_copy(prec, pwin.at[pl.ds(8, 32)], loc_sem.at[4]),
-        pltpu.make_async_copy(pick.at[pl.ds(pl.multiple_of(n // 8 * 8, 8), 8)], picked, loc_sem.at[5]),
-        pltpu.make_async_copy(taper, tap, loc_sem.at[6]),
+        pltpu.make_async_copy(small.at[pl.ds(0, 32)], vwin.at[pl.ds(8, 32)], loc_sem.at[3]),
+        pltpu.make_async_copy(small.at[pl.ds(32, 32)], pwin.at[pl.ds(8, 32)], loc_sem.at[4]),
+        pltpu.make_async_copy(small.at[pl.ds(64, 16)], picks, loc_sem.at[5]),
     ]
     for copy in smalls:
         copy.start()
@@ -102,68 +98,89 @@
 
     send_states(0)
 
-    def move(slot, count, index, sem):
-        block = win.at[rows(slot, count)]
-        return remote(block, block, obs_send.at[sem], obs_recv.at[sem], (w, index))
-
-    other_core, _ = at(0, 0, 1)
-    x_peer, _ = at(0, 1, 0)
-    up, _ = at(1, 0, 0)
-    down, _ = at(3, 0, 0)
+    left, right = (0, WIN // 2), (WIN // 2, WIN // 2)
+    right_low, right_high = (WIN // 2, WIN // 4), (WIN // 2 + WIN // 4, WIN // 4)
+
+    def move(slot, count, columns, to, sem):
+        block = win.at[rows(slot, count), pl.ds(*columns)]
+        copy = remote(block, block, obs_send.at[sem], obs_recv.at[sem], (w, at(*to)[0]))
+        copy.start()
+        moves.append(copy)
+        return copy
 
     def pair(dy):
         return 4 * ((y + dy) % 4) + 2 * c
 
+    def one(dy):
+        return pair(dy) + x
+
+    moves = []
+    up, down, across, core = (1, 0, 0), (3, 0, 0), (0, 1, 0), (0, 0, 1)
     own_obs.wait()
     halos[0].wait_recv()
     for copy in halos[1::2]:
         copy.start()
+    left_x = move(one(0), 1, left, across, 0)
+    send_states(1)
     halos[1].wait_recv()
-    to_x = move(me, 1, x_peer, 0)
-    to_x.start()
-    send_states(1)
-    to_x.wait_recv()
-    to_up = move(pair(0), 2, up, 1)
-    to_down = move(pair(0), 2, down, 2)
-    to_core0 = move(pair(0), 2, other_core, 3)
-    to_up.start()
-    to_down.start()
-    to_core0.start()
+    right_up = move(one(0), 1, right, up, 1)
+    right_down = move(one(0), 1, right, down, 2)
+    right_x0 = move(one(0), 1, right, across, 3)
+    left_x.wait_recv()
+    left_up = move(pair(0), 2, left, up, 4)
+    left_down = move(pair(0), 2, left, down, 5)
+    last = [move(pair(0), 2, left, core, 6)]
     send_states(2)
-    to_up.wait_recv()
-    on_up = move(pair(3), 1, up, 4)
-    on_up.start()
-    to_core1 = move(pair(3), 2, other_core, 5)
-    to_core1.start()
-    to_down.wait_recv()
-    on_down = move(pair(1) + 1, 1, down, 6)
-    on_down.start()
-    to_core2 = move(pair(1), 2, other_core, 7)
-    to_core2.start()
+    right_up.wait_recv()
+    right_up2 = move(one(3), 1, right_low, up, 7)
+    right_x3 = move(one(3), 1, right, across, 8)
+    right_down.wait_recv()
+    right_down2 = move(one(1), 1, right_high, down, 9)
+    right_x1 = move(one(1), 1, right, across, 10)
+    left_up.wait_recv()
+    left_up2 = move(pair(3), 1, left, up, 11)
+    last.append(move(pair(3), 2, left, core, 12))
+    left_down.wait_recv()
+    left_down2 = move(pair(1) + 1, 1, left, down, 13)
+    last.append(move(pair(1), 2, left, core, 14))
     send_states(3)
-    on_up.wait_recv()
-    on_down.wait_recv()
-    to_core3 = move(pair(2), 2, other_core, 8)
-    to_core3.start()
-
-    @pl.loop(4, CHUNKS)
+    right_up2.wait_recv()
+    right_down2.wait_recv()
+    right_x2 = move(one(2), 1, right, across, 15)
+    right_x0.wait_recv()
+    last.append(move(pair(0), 2, right, core, 16))
+    right_x3.wait_recv()
+    last.append(move(pair(3), 2, right, core, 17))
+    right_x1.wait_recv()
+    last.append(move(pair(1), 2, right, core, 18))
+    left_up2.wait_recv()
+    left_down2.wait_recv()
+    last.append(move(pair(2), 2, left, core, 19))
+    send_states(4)
+    right_x2.wait_recv()
+    last.append(move(pair(2), 2, right, core, 20))
+
+    @pl.loop(5, CHUNKS)
     def _(chunk):
         send_states(chunk)
 
     for copy in smalls:
         copy.wait()
-    own_pick = picked[pl.ds(n % 8, 1), :]
+    own_taper, own_pick = (
+        jnp.concatenate([picks[8 * part + k : 8 * part + k + 1, :] for k in range(8)], axis=1) for part in (0, 1)
+    )
+    own_pick = own_pick.astype(jnp.int32)
     coarse = lax.broadcasted_iota(jnp.int32, (40, NPICK), 0) == (own_pick >> 7)
     fine = lax.broadcasted_iota(jnp.int32, (LANES, NPICK), 0) == (own_pick & 127)
     tapwin[...] = lax.dot_general(
-        jnp.where(coarse, tap[...], 0.0), fine.astype(jnp.float32), NT,
+        jnp.where(coarse, own_taper, 0.0), fine.astype(jnp.float32), NT,
         precision=HIGH, preferred_element_type=jnp.float32,
     )
     gram[...] = jnp.zeros_like(gram)
     facc[...] = jnp.zeros_like(facc)
     for copy in halos[2:]:
         copy.wait_recv()
-    for copy in (to_core0, to_core1, to_core2, to_core3):
+    for copy in last:
         copy.wait_recv()
 
     @pl.loop(0, WIN // TILE)
@@ -240,7 +257,7 @@
     own_out.start()
     for copy in halos:
         copy.wait_send()
-    for copy in (to_x, to_up, to_down, on_up, on_down, to_core0, to_core1, to_core2, to_core3):
+    for copy in moves:
         copy.wait_send()
 
     @pl.loop(0, CHUNKS)
@@ -257,10 +274,14 @@
 def body(states, obs_ens, obs_value, obs_prec, obs_pick, taper):
     hbm, anywhere = (pl.BlockSpec(memory_space=pltpu.HBM), pl.BlockSpec(memory_space=pl.ANY))
     dma = pltpu.SemaphoreType.DMA
+    own_pick = lax.dynamic_slice_in_dim(obs_pick, lax.axis_index("narrow"), 1, 0)
+    small = jnp.concatenate(
+        [part.astype(jnp.float32).reshape(-1, LANES) for part in (obs_value, obs_prec, taper, own_pick)], axis=0
+    )
     return pl.pallas_call(
         kernel,
         out_shape=jax.ShapeDtypeStruct(states.shape, jnp.bfloat16),
-        in_specs=[hbm] * 6,
+        in_specs=[hbm] * 3,
         out_specs=anywhere,
         scratch_shapes=[
             pltpu.VMEM((MEMBERS, CELLS), jnp.bfloat16),
@@ -268,8 +289,7 @@
             pltpu.VMEM((MEMBERS, WIN), jnp.bfloat16),
             pltpu.VMEM((48, LANES), jnp.float32),
             pltpu.VMEM((48, LANES), jnp.float32),
-            pltpu.VMEM((8, NPICK), jnp.int32),
-            pltpu.VMEM((1, NPICK), jnp.float32),
+            pltpu.VMEM((16, LANES), jnp.float32),
             pltpu.VMEM((40, LANES), jnp.float32),
             pltpu.VMEM((MEMBERS, MEMBERS), jnp.float32),
             pltpu.VMEM((MEMBERS, LANES), jnp.float32),
@@ -278,17 +298,17 @@
             dma((CHUNKS,)),
             dma((CHUNKS,)),
             dma((CHUNKS,)),
-            dma((7,)),
             dma((6,)),
             dma((6,)),
-            dma((9,)),
-            dma((9,)),
+            dma((6,)),
+            dma((21,)),
+            dma((21,)),
         ],
         compiler_params=pltpu.CompilerParams(
             collective_id=0, has_side_effects=True, vmem_limit_bytes=48 << 20
         ),
         name="analysis",
-    )(states, obs_ens, obs_value.reshape(OBS_W // LANES, LANES), obs_prec.reshape(OBS_W // LANES, LANES), obs_pick, taper)
+    )(states, obs_ens, small)
 
 
 def solution(mesh):

time: 121 us -> 113 us (0.934)
  the two profiles are of different devices: /device:TPU:103 before, /device:TPU:1 now
where the time goes in v3:
time: 113 us
  Pallas kernels  109 us (96%)
  local copies, waits for them, and re-layouts  2.92 us (3%)
  other arithmetic  1.52 us (1%)
    pallas_call x1, Pallas kernels, body(): pl.pallas_call(kernel, out_shape=jax.ShapeDtypeStruct(states.shape, jnp.b...  109 us
    unnamed x3, local copies, waits for them, and re-layouts  2.92 us

profile of v3, /device:TPU:1, one launch (start us, length us, event | category | flops | bytes accessed | tf_op | source)
XLA Modules:
  0.0 113.1 jit_solution(5780703529000147454)
XLA Ops:
  0.0 0.8 dynamic-slice_convert_fusion
  0.8 0.8 pad_maximum_fusion.small
  1.5 0.0 copy-start
  1.5 0.9 copy-done
  2.4 108.7 %analysis.1 = bf16[16,131072]{1,0:T(8,128)(2,1)S(1)} custom-call(bf16[16,131072]{1,0:T(8,128)(2,1)} %states.1, bf16[16,4096]{1,0:T(8,128)(2,1)S(1)} %copy-done, f32[80,128]{1,0:T(8,128)S(1)} %pad_maximum_fusion.small), custom_call_target="tpu_custom_call" | custom-call | tf_op jit(solution)/shard_map/analysis/pallas_call | solution.py:281
  111.1 2.0 %copy.8 = bf16[16,131072]{1,0:T(8,128)(2,1)} copy(bf16[16,131072]{1,0:T(8,128)(2,1)S(1)} %analysis.1) | data formatting | bytes 8388608
Async XLA Ops:
  1.5 0.9 copy-start

commit v4 on v3

--- a/solution.py
+++ b/solution.py
@@ -23,6 +23,9 @@
 CHUNKS = 8
 CHUNK = CELLS // CHUNKS
 TILE = 256
+LEFT = 2560
+VALUE_ROW, PREC_ROW, TAPER_ROW = 0, OBS_W // LANES, 2 * OBS_W // LANES
+PICK_ROW = TAPER_ROW + NPICK // LANES
 MESH = pl.DeviceIdType.MESH
 HIGH = lax.Precision.HIGHEST
 NT = (((1,), (1,)), ((), ()))
@@ -34,7 +37,7 @@
 
 
 def kernel(states, obs, small, out,
-           inbuf, outbuf, win, vwin, pwin, picks, tapwin, gram, facc, trans,
+           inbuf, outbuf, win, vwin, pwin, tapwin, gram, facc, trans,
            in_send, in_recv, out_send, out_recv, loc_sem, halo_send, halo_recv, obs_send, obs_recv):
     w = lax.axis_index("wide")
     n = lax.axis_index("narrow")
@@ -55,6 +58,15 @@
     for index, _ in peers:
         pl.semaphore_signal(barrier, inc=1, device_id=(w, index), device_id_type=MESH)
     pl.semaphore_signal(barrier, inc=1, device_id=(before, n), device_id_type=MESH)
+
+    mine = rows(me)
+    win[mine, 0:OBS_W] = obs[...]
+    vwin[0:32] = small[VALUE_ROW : VALUE_ROW + 32, :]
+    pwin[0:32] = small[PREC_ROW : PREC_ROW + 32, :]
+    own_states = pltpu.make_async_copy(
+        states.at[:, pl.ds(pl.multiple_of(n * CELLS, CELLS), CELLS)], inbuf.at[mine], loc_sem.at[0]
+    )
+    own_states.start()
     pl.semaphore_wait(barrier, len(PEERS) + 1)
 
     def remote(src, dst, send, recv, device):
@@ -62,31 +74,17 @@
             src_ref=src, dst_ref=dst, send_sem=send, recv_sem=recv, device_id=device, device_id_type=MESH
         )
 
-    mine = rows(me)
     halos = [
-        remote(obs.at[:, pl.ds(OBS_W - HALO, HALO)], win.at[mine, pl.ds(0, HALO)],
+        remote(win.at[mine, pl.ds(OBS_W - HALO, HALO)], win.at[mine, pl.ds(OBS_W, HALO)],
                halo_send.at[0], halo_recv.at[0], (after, n)),
-        remote(obs.at[:, pl.ds(0, HALO)], win.at[mine, pl.ds(HALO + OBS_W, HALO)],
+        remote(win.at[mine, pl.ds(0, HALO)], win.at[mine, pl.ds(OBS_W + HALO, HALO)],
                halo_send.at[1], halo_recv.at[1], (before, n)),
-        remote(small.at[pl.ds(24, 8)], vwin.at[pl.ds(0, 8)], halo_send.at[2], halo_recv.at[2], (after, n)),
-        remote(small.at[pl.ds(0, 8)], vwin.at[pl.ds(40, 8)], halo_send.at[3], halo_recv.at[3], (before, n)),
-        remote(small.at[pl.ds(56, 8)], pwin.at[pl.ds(0, 8)], halo_send.at[4], halo_recv.at[4], (after, n)),
-        remote(small.at[pl.ds(32, 8)], pwin.at[pl.ds(40, 8)], halo_send.at[5], halo_recv.at[5], (before, n)),
+        remote(small.at[pl.ds(VALUE_ROW + 24, 8)], vwin.at[pl.ds(32, 8)], halo_send.at[2], halo_recv.at[2], (after, n)),
+        remote(small.at[pl.ds(VALUE_ROW, 8)], vwin.at[pl.ds(40, 8)], halo_send.at[3], halo_recv.at[3], (before, n)),
+        remote(small.at[pl.ds(PREC_ROW + 24, 8)], pwin.at[pl.ds(32, 8)], halo_send.at[4], halo_recv.at[4], (after, n)),
+        remote(small.at[pl.ds(PREC_ROW, 8)], pwin.at[pl.ds(40, 8)], halo_send.at[5], halo_recv.at[5], (before, n)),
     ]
     for copy in halos[0::2]:
-        copy.start()
-    own_obs = pltpu.make_async_copy(obs, win.at[mine, pl.ds(HALO, OBS_W)], loc_sem.at[0])
-    own_obs.start()
-    own_states = pltpu.make_async_copy(
-        states.at[:, pl.ds(pl.multiple_of(n * CELLS, CELLS), CELLS)], inbuf.at[mine], loc_sem.at[1]
-    )
-    own_states.start()
-    smalls = [
-        pltpu.make_async_copy(small.at[pl.ds(0, 32)], vwin.at[pl.ds(8, 32)], loc_sem.at[3]),
-        pltpu.make_async_copy(small.at[pl.ds(32, 32)], pwin.at[pl.ds(8, 32)], loc_sem.at[4]),
-        pltpu.make_async_copy(small.at[pl.ds(64, 16)], picks, loc_sem.at[5]),
-    ]
-    for copy in smalls:
         copy.start()
 
     def send_states(chunk):
@@ -96,12 +94,13 @@
                    inbuf.at[mine, pl.ds(pl.multiple_of(chunk * CHUNK, CHUNK), CHUNK)],
                    in_send.at[chunk], in_recv.at[chunk], (w, index)).start()
 
-    send_states(0)
-
-    left, right = (0, WIN // 2), (WIN // 2, WIN // 2)
-    right_low, right_high = (WIN // 2, WIN // 4), (WIN // 2 + WIN // 4, WIN // 4)
-
-    def move(slot, count, columns, to, sem):
+    left, right = (0, LEFT), (LEFT, WIN - LEFT)
+    half = (WIN - LEFT) // 2
+    right_low, right_high = (LEFT, half), (LEFT + half, half)
+    moves = []
+
+    def move(slot, count, columns, to):
+        sem = len(moves)
         block = win.at[rows(slot, count), pl.ds(*columns)]
         copy = remote(block, block, obs_send.at[sem], obs_recv.at[sem], (w, at(*to)[0]))
         copy.start()
@@ -114,62 +113,60 @@
     def one(dy):
         return pair(dy) + x
 
-    moves = []
     up, down, across, core = (1, 0, 0), (3, 0, 0), (0, 1, 0), (0, 0, 1)
-    own_obs.wait()
+    left_x = move(one(0), 1, left, across)
+    send_states(0)
+    left_x.wait_recv()
+    left_up = move(pair(0), 2, left, up)
+    left_down = move(pair(0), 2, left, down)
+    last = [move(pair(0), 2, left, core)]
     halos[0].wait_recv()
     for copy in halos[1::2]:
         copy.start()
-    left_x = move(one(0), 1, left, across, 0)
     send_states(1)
     halos[1].wait_recv()
-    right_up = move(one(0), 1, right, up, 1)
-    right_down = move(one(0), 1, right, down, 2)
-    right_x0 = move(one(0), 1, right, across, 3)
-    left_x.wait_recv()
-    left_up = move(pair(0), 2, left, up, 4)
-    left_down = move(pair(0), 2, left, down, 5)
-    last = [move(pair(0), 2, left, core, 6)]
+    right_up = move(one(0), 1, right, up)
+    right_down = move(one(0), 1, right, down)
+    right_x0 = move(one(0), 1, right, across)
+    left_up.wait_recv()
+    left_up2 = move(pair(3), 1, left, up)
+    last.append(move(pair(3), 2, left, core))
+    left_down.wait_recv()
+    left_down2 = move(pair(1) + 1, 1, left, down)
+    last.append(move(pair(1), 2, left, core))
     send_states(2)
     right_up.wait_recv()
-    right_up2 = move(one(3), 1, right_low, up, 7)
-    right_x3 = move(one(3), 1, right, across, 8)
+    right_up2 = move(one(3), 1, right_low, up)
+    right_x3 = move(one(3), 1, right, across)
     right_down.wait_recv()
-    right_down2 = move(one(1), 1, right_high, down, 9)
-    right_x1 = move(one(1), 1, right, across, 10)
-    left_up.wait_recv()
-    left_up2 = move(pair(3), 1, left, up, 11)
-    last.append(move(pair(3), 2, left, core, 12))
-    left_down.wait_recv()
-    left_down2 = move(pair(1) + 1, 1, left, down, 13)
-    last.append(move(pair(1), 2, left, core, 14))
+    right_down2 = move(one(1), 1, right_high, down)
+    right_x1 = move(one(1), 1, right, across)
+    left_up2.wait_recv()
+    left_down2.wait_recv()
+    last.append(move(pair(2), 2, left, core))
     send_states(3)
     right_up2.wait_recv()
     right_down2.wait_recv()
-    right_x2 = move(one(2), 1, right, across, 15)
+    right_x2 = move(one(2), 1, right, across)
     right_x0.wait_recv()
-    last.append(move(pair(0), 2, right, core, 16))
+    last.append(move(pair(0), 2, right, core))
     right_x3.wait_recv()
-    last.append(move(pair(3), 2, right, core, 17))
+    last.append(move(pair(3), 2, right, core))
     right_x1.wait_recv()
-    last.append(move(pair(1), 2, right, core, 18))
-    left_up2.wait_recv()
-    left_down2.wait_recv()
-    last.append(move(pair(2), 2, left, core, 19))
+    last.append(move(pair(1), 2, right, core))
     send_states(4)
     right_x2.wait_recv()
-    last.append(move(pair(2), 2, right, core, 20))
+    last.append(move(pair(2), 2, right, core))
 
     @pl.loop(5, CHUNKS)
     def _(chunk):
         send_states(chunk)
 
-    for copy in smalls:
-        copy.wait()
-    own_taper, own_pick = (
-        jnp.concatenate([picks[8 * part + k : 8 * part + k + 1, :] for k in range(8)], axis=1) for part in (0, 1)
-    )
-    own_pick = own_pick.astype(jnp.int32)
+    own_taper = jnp.concatenate([small[TAPER_ROW + k : TAPER_ROW + k + 1, :] for k in range(8)], axis=1)
+    own_pick = jnp.concatenate([small[PICK_ROW + k : PICK_ROW + k + 1, :] for k in range(8)], axis=1).astype(jnp.int32)
+    own_pick = jnp.where(
+        own_pick < HALO, own_pick + OBS_W, jnp.where(own_pick < HALO + OBS_W, own_pick - HALO, own_pick)
+    )
     coarse = lax.broadcasted_iota(jnp.int32, (40, NPICK), 0) == (own_pick >> 7)
     fine = lax.broadcasted_iota(jnp.int32, (LANES, NPICK), 0) == (own_pick & 127)
     tapwin[...] = lax.dot_general(
@@ -188,7 +185,7 @@
         columns = pl.ds(pl.multiple_of(tile * TILE, TILE), TILE)
 
         def flat(ref, first):
-            row = first + 2 * tile
+            row = 2 * tile + first * (tile // (OBS_W // TILE))
             return jnp.concatenate([ref[pl.ds(row, 1), :], ref[pl.ds(row + 1, 1), :]], axis=1)
 
         ensemble = win[:, columns].astype(jnp.float32)
@@ -210,17 +207,20 @@
 
     matrix = gram[...] + (MEMBERS - 1.0) * identity
     scale = jnp.sqrt(jnp.sum(jnp.sum(matrix * matrix, axis=0, keepdims=True), axis=1, keepdims=True))
-    gram[...] = matrix / scale
-    trans[...] = identity
-
-    @pl.loop(0, ITERS)
+    start = matrix / scale
+    first = 1.5 * identity - 0.5 * start
+    gram[...] = dot(start, first)
+    trans[...] = first
+
+    @pl.loop(0, ITERS - 2)
     def _(_):
         current, root = gram[...], trans[...]
         middle = 1.5 * identity - 0.5 * dot(root, current)
         gram[...] = dot(current, middle)
         trans[...] = dot(middle, root)
 
-    inv_root = trans[...] / jnp.sqrt(scale)
+    root = dot(1.5 * identity - 0.5 * dot(trans[...], gram[...]), trans[...])
+    inv_root = root / jnp.sqrt(scale)
     force = lax.dot_general(
         jnp.ones((8, LANES), jnp.float32), facc[...], NT, precision=HIGH, preferred_element_type=jnp.float32
     )
@@ -252,7 +252,7 @@
                    out_send.at[chunk], out_recv.at[chunk], (w, index)).start()
 
     own_out = pltpu.make_async_copy(
-        outbuf.at[mine], out.at[:, pl.ds(pl.multiple_of(n * CELLS, CELLS), CELLS)], loc_sem.at[2]
+        outbuf.at[mine], out.at[:, pl.ds(pl.multiple_of(n * CELLS, CELLS), CELLS)], loc_sem.at[1]
     )
     own_out.start()
     for copy in halos:
@@ -272,8 +272,9 @@
 
 
 def body(states, obs_ens, obs_value, obs_prec, obs_pick, taper):
-    hbm, anywhere = (pl.BlockSpec(memory_space=pltpu.HBM), pl.BlockSpec(memory_space=pl.ANY))
+    vmem, anywhere = (pl.BlockSpec(memory_space=pltpu.VMEM), pl.BlockSpec(memory_space=pl.ANY))
     dma = pltpu.SemaphoreType.DMA
+
     own_pick = lax.dynamic_slice_in_dim(obs_pick, lax.axis_index("narrow"), 1, 0)
     small = jnp.concatenate(
         [part.astype(jnp.float32).reshape(-1, LANES) for part in (obs_value, obs_prec, taper, own_pick)], axis=0
@@ -281,7 +282,7 @@
     return pl.pallas_call(
         kernel,
         out_shape=jax.ShapeDtypeStruct(states.shape, jnp.bfloat16),
-        in_specs=[hbm] * 3,
+        in_specs=[anywhere, vmem, vmem],
         out_specs=anywhere,
         scratch_shapes=[
             pltpu.VMEM((MEMBERS, CELLS), jnp.bfloat16),
@@ -289,7 +290,6 @@
             pltpu.VMEM((MEMBERS, WIN), jnp.bfloat16),
             pltpu.VMEM((48, LANES), jnp.float32),
             pltpu.VMEM((48, LANES), jnp.float32),
-            pltpu.VMEM((16, LANES), jnp.float32),
             pltpu.VMEM((40, LANES), jnp.float32),
             pltpu.VMEM((MEMBERS, MEMBERS), jnp.float32),
             pltpu.VMEM((MEMBERS, LANES), jnp.float32),
@@ -298,7 +298,7 @@
             dma((CHUNKS,)),
             dma((CHUNKS,)),
             dma((CHUNKS,)),
-            dma((6,)),
+            dma((2,)),
             dma((6,)),
             dma((6,)),
             dma((21,)),

time: 113 us -> 111 us (0.982)
  Pallas kernels: 109 us -> 106 us
    pallas_call x1, Pallas kernels: 109 us -> 106 us  [body(): pl.pallas_call(kernel, out_shape=jax.ShapeDtypeStruct(states.shape, jnp.b...]
where the time goes in v4:
time: 111 us; the launch traced here: 110 us
  Pallas kernels  106 us (95%)
  local copies, waits for them, and re-layouts  2.92 us (3%)
  other arithmetic  1.52 us (1%)
    pallas_call x1, Pallas kernels, body(): pl.pallas_call(kernel, out_shape=jax.ShapeDtypeStruct(states.shape, jnp.b...  106 us
    unnamed x3, local copies, waits for them, and re-layouts  2.92 us

profile of v4, /device:TPU:1, one launch (start us, length us, event | category | flops | bytes accessed | tf_op | source)
XLA Modules:
  0.0 110.1 jit_solution(4337325058312757111)
XLA Ops:
  0.0 0.8 dynamic-slice_convert_fusion
  0.8 0.8 pad_maximum_fusion.small
  1.5 0.0 copy-start
  1.5 0.9 copy-done
  2.4 105.7 %analysis.1 = bf16[16,131072]{1,0:T(8,128)(2,1)S(1)} custom-call(bf16[16,131072]{1,0:T(8,128)(2,1)} %states.1, bf16[16,4096]{1,0:T(8,128)(2,1)S(1)} %copy-done, f32[80,128]{1,0:T(8,128)S(1)} %pad_maximum_fusion.small), custom_call_target="tpu_custom_call" | custom-call | tf_op jit(solution)/shard_map/analysis/pallas_call | solution.py:282
  108.1 2.0 %copy.8 = bf16[16,131072]{1,0:T(8,128)(2,1)} copy(bf16[16,131072]{1,0:T(8,128)(2,1)S(1)} %analysis.1) | data formatting | bytes 8388608
Async XLA Ops:
  1.5 0.9 copy-start

commit v5 on v4

--- a/solution.py
+++ b/solution.py
@@ -1,4 +1,3 @@
-import functools
 import math
 
 import jax
@@ -17,15 +16,11 @@
 NPICK = 1024
 ITERS = 6
 N_WIDE = 16
-N_NARROW = 16
 LANES = 128
-WIN_ROWS = WIN // LANES
 CHUNKS = 8
 CHUNK = CELLS // CHUNKS
 TILE = 256
 LEFT = 2560
-VALUE_ROW, PREC_ROW, TAPER_ROW = 0, OBS_W // LANES, 2 * OBS_W // LANES
-PICK_ROW = TAPER_ROW + NPICK // LANES
 MESH = pl.DeviceIdType.MESH
 HIGH = lax.Precision.HIGHEST
 NT = (((1,), (1,)), ((), ()))
@@ -36,8 +31,8 @@
 ]
 
 
-def kernel(states, obs, small, out,
-           inbuf, outbuf, win, vwin, pwin, tapwin, gram, facc, trans,
+def kernel(states, obs, value, prec, pick, taper, out,
+           inbuf, outbuf, win, vwin, pwin, picked, tap, tapwin, gram, facc, trans,
            in_send, in_recv, out_send, out_recv, loc_sem, halo_send, halo_recv, obs_send, obs_recv):
     w = lax.axis_index("wide")
     n = lax.axis_index("narrow")
@@ -60,9 +55,15 @@
     pl.semaphore_signal(barrier, inc=1, device_id=(before, n), device_id_type=MESH)
 
     mine = rows(me)
-    win[mine, 0:OBS_W] = obs[...]
-    vwin[0:32] = small[VALUE_ROW : VALUE_ROW + 32, :]
-    pwin[0:32] = small[PREC_ROW : PREC_ROW + 32, :]
+    locals_ = [
+        pltpu.make_async_copy(obs, win.at[mine, pl.ds(0, OBS_W)], loc_sem.at[2]),
+        pltpu.make_async_copy(value, vwin.at[pl.ds(0, 32)], loc_sem.at[3]),
+        pltpu.make_async_copy(prec, pwin.at[pl.ds(0, 32)], loc_sem.at[4]),
+        pltpu.make_async_copy(pick.at[pl.ds(pl.multiple_of(n // 8 * 8, 8), 8)], picked, loc_sem.at[5]),
+        pltpu.make_async_copy(taper, tap, loc_sem.at[6]),
+    ]
+    for copy in locals_:
+        copy.start()
     own_states = pltpu.make_async_copy(
         states.at[:, pl.ds(pl.multiple_of(n * CELLS, CELLS), CELLS)], inbuf.at[mine], loc_sem.at[0]
     )
@@ -75,14 +76,14 @@
         )
 
     halos = [
-        remote(win.at[mine, pl.ds(OBS_W - HALO, HALO)], win.at[mine, pl.ds(OBS_W, HALO)],
+        remote(obs.at[:, pl.ds(OBS_W - HALO, HALO)], win.at[mine, pl.ds(OBS_W, HALO)],
                halo_send.at[0], halo_recv.at[0], (after, n)),
-        remote(win.at[mine, pl.ds(0, HALO)], win.at[mine, pl.ds(OBS_W + HALO, HALO)],
+        remote(obs.at[:, pl.ds(0, HALO)], win.at[mine, pl.ds(OBS_W + HALO, HALO)],
                halo_send.at[1], halo_recv.at[1], (before, n)),
-        remote(small.at[pl.ds(VALUE_ROW + 24, 8)], vwin.at[pl.ds(32, 8)], halo_send.at[2], halo_recv.at[2], (after, n)),
-        remote(small.at[pl.ds(VALUE_ROW, 8)], vwin.at[pl.ds(40, 8)], halo_send.at[3], halo_recv.at[3], (before, n)),
-        remote(small.at[pl.ds(PREC_ROW + 24, 8)], pwin.at[pl.ds(32, 8)], halo_send.at[4], halo_recv.at[4], (after, n)),
-        remote(small.at[pl.ds(PREC_ROW, 8)], pwin.at[pl.ds(40, 8)], halo_send.at[5], halo_recv.at[5], (before, n)),
+        remote(value.at[pl.ds(24, 8)], vwin.at[pl.ds(32, 8)], halo_send.at[2], halo_recv.at[2], (after, n)),
+        remote(value.at[pl.ds(0, 8)], vwin.at[pl.ds(40, 8)], halo_send.at[3], halo_recv.at[3], (before, n)),
+        remote(prec.at[pl.ds(24, 8)], pwin.at[pl.ds(32, 8)], halo_send.at[4], halo_recv.at[4], (after, n)),
+        remote(prec.at[pl.ds(0, 8)], pwin.at[pl.ds(40, 8)], halo_send.at[5], halo_recv.at[5], (before, n)),
     ]
     for copy in halos[0::2]:
         copy.start()
@@ -114,6 +115,7 @@
         return pair(dy) + x
 
     up, down, across, core = (1, 0, 0), (3, 0, 0), (0, 1, 0), (0, 0, 1)
+    locals_[0].wait()
     left_x = move(one(0), 1, left, across)
     send_states(0)
     left_x.wait_recv()
@@ -162,15 +164,16 @@
     def _(chunk):
         send_states(chunk)
 
-    own_taper = jnp.concatenate([small[TAPER_ROW + k : TAPER_ROW + k + 1, :] for k in range(8)], axis=1)
-    own_pick = jnp.concatenate([small[PICK_ROW + k : PICK_ROW + k + 1, :] for k in range(8)], axis=1).astype(jnp.int32)
+    for copy in locals_[1:]:
+        copy.wait()
+    own_pick = picked[pl.ds(n % 8, 1), :]
     own_pick = jnp.where(
         own_pick < HALO, own_pick + OBS_W, jnp.where(own_pick < HALO + OBS_W, own_pick - HALO, own_pick)
     )
     coarse = lax.broadcasted_iota(jnp.int32, (40, NPICK), 0) == (own_pick >> 7)
     fine = lax.broadcasted_iota(jnp.int32, (LANES, NPICK), 0) == (own_pick & 127)
     tapwin[...] = lax.dot_general(
-        jnp.where(coarse, own_taper, 0.0), fine.astype(jnp.float32), NT,
+        jnp.where(coarse, tap[...], 0.0), fine.astype(jnp.float32), NT,
         precision=HIGH, preferred_element_type=jnp.float32,
     )
     gram[...] = jnp.zeros_like(gram)
@@ -272,17 +275,13 @@
 
 
 def body(states, obs_ens, obs_value, obs_prec, obs_pick, taper):
-    vmem, anywhere = (pl.BlockSpec(memory_space=pltpu.VMEM), pl.BlockSpec(memory_space=pl.ANY))
+    anywhere = pl.BlockSpec(memory_space=pl.ANY)
     dma = pltpu.SemaphoreType.DMA
 
-    own_pick = lax.dynamic_slice_in_dim(obs_pick, lax.axis_index("narrow"), 1, 0)
-    small = jnp.concatenate(
-        [part.astype(jnp.float32).reshape(-1, LANES) for part in (obs_value, obs_prec, taper, own_pick)], axis=0
-    )
     return pl.pallas_call(
         kernel,
         out_shape=jax.ShapeDtypeStruct(states.shape, jnp.bfloat16),
-        in_specs=[anywhere, vmem, vmem],
+        in_specs=[anywhere] * 6,
         out_specs=anywhere,
         scratch_shapes=[
             pltpu.VMEM((MEMBERS, CELLS), jnp.bfloat16),
@@ -290,6 +289,8 @@
             pltpu.VMEM((MEMBERS, WIN), jnp.bfloat16),
             pltpu.VMEM((48, LANES), jnp.float32),
             pltpu.VMEM((48, LANES), jnp.float32),
+            pltpu.VMEM((8, NPICK), jnp.int32),
+            pltpu.VMEM((1, NPICK), jnp.float32),
             pltpu.VMEM((40, LANES), jnp.float32),
             pltpu.VMEM((MEMBERS, MEMBERS), jnp.float32),
             pltpu.VMEM((MEMBERS, LANES), jnp.float32),
@@ -298,7 +299,7 @@
             dma((CHUNKS,)),
             dma((CHUNKS,)),
             dma((CHUNKS,)),
-            dma((2,)),
+            dma((7,)),
             dma((6,)),
             dma((6,)),
             dma((21,)),
@@ -308,7 +309,14 @@
             collective_id=0, has_side_effects=True, vmem_limit_bytes=48 << 20
         ),
         name="analysis",
-    )(states, obs_ens, small)
+    )(*(pltpu.with_memory_space_constraint(a, pltpu.HBM) for a in (
+        states,
+        obs_ens,
+        obs_value.reshape(OBS_W // LANES, LANES),
+        obs_prec.reshape(OBS_W // LANES, LANES),
+        obs_pick,
+        taper,
+    )))
 
 
 def solution(mesh):

time: 111 us -> 108 us (0.973)
  other arithmetic: 1.52 us -> 0 us
    unnamed x3 -> x1, local copies, waits for them, and re-layouts: 2.92 us -> 2.02 us
where the time goes in v5:
time: 108 us
  Pallas kernels  106 us (98%)
  local copies, waits for them, and re-layouts  2.02 us (2%)
    pallas_call x1, Pallas kernels, body(): pl.pallas_call(kernel, out_shape=jax.ShapeDtypeStruct(states.shape, jnp.b...  106 us

profile of v5, /device:TPU:1, one launch (start us, length us, event | category | flops | bytes accessed | tf_op | source)
XLA Modules:
  0.0 108.0 jit_solution(10764220809532030240)
XLA Ops:
  0.0 106.0 %analysis.1 = bf16[16,131072]{1,0:T(8,128)(2,1)S(1)} custom-call(bf16[16,131072]{1,0:T(8,128)(2,1)} %states.1, bf16[16,4096]{1,0:T(8,128)(2,1)} %obs.1, f32[32,128]{1,0:T(8,128)} %bitcast.2, f32[32,128]{1,0:T(8,128)} %bitcast.3, s32[16,1024]{1,0:T(8,128)} %pick.1, f32[1,1024]{1,0:T(1,128)} %taper.1), custom_call_target="tpu_custom_call" | custom-call | tf_op jit(solution)/shard_map/analysis/pallas_call | solution.py:281
  106.0 2.0 %copy.8 = bf16[16,131072]{1,0:T(8,128)(2,1)} copy(bf16[16,131072]{1,0:T(8,128)(2,1)S(1)} %analysis.1) | data formatting | bytes 8388608

commit v6 on v5

--- a/solution.py
+++ b/solution.py
@@ -52,7 +52,16 @@
     barrier = pltpu.get_barrier_semaphore()
     for index, _ in peers:
         pl.semaphore_signal(barrier, inc=1, device_id=(w, index), device_id_type=MESH)
-    pl.semaphore_signal(barrier, inc=1, device_id=(before, n), device_id_type=MESH)
+    first_band, last_band = w == 0, w == N_WIDE - 1
+
+    @pl.when(jnp.logical_not(last_band))
+    def _():
+        pl.semaphore_signal(barrier, inc=1, device_id=(after, n), device_id_type=MESH)
+
+    @pl.when(first_band)
+    def _():
+        pl.semaphore_signal(barrier, inc=1, device_id=(before, n), device_id_type=MESH)
+
 
     mine = rows(me)
     locals_ = [
@@ -68,7 +77,7 @@
         states.at[:, pl.ds(pl.multiple_of(n * CELLS, CELLS), CELLS)], inbuf.at[mine], loc_sem.at[0]
     )
     own_states.start()
-    pl.semaphore_wait(barrier, len(PEERS) + 1)
+    pl.semaphore_wait(barrier, len(PEERS) + jnp.where(first_band, 0, jnp.where(last_band, 2, 1)))
 
     def remote(src, dst, send, recv, device):
         return pltpu.make_async_remote_copy(
@@ -85,8 +94,16 @@
         remote(prec.at[pl.ds(24, 8)], pwin.at[pl.ds(32, 8)], halo_send.at[4], halo_recv.at[4], (after, n)),
         remote(prec.at[pl.ds(0, 8)], pwin.at[pl.ds(40, 8)], halo_send.at[5], halo_recv.at[5], (before, n)),
     ]
-    for copy in halos[0::2]:
-        copy.start()
+    to_after, to_before = halos[0::2], halos[1::2]
+
+    def start_if(condition, copies):
+        @pl.when(condition)
+        def _():
+            for copy in copies:
+                copy.start()
+
+    start_if(jnp.logical_not(first_band), to_before)
+    start_if(last_band, to_after)
 
     def send_states(chunk):
         for index, _ in peers:
@@ -122,11 +139,11 @@
     left_up = move(pair(0), 2, left, up)
     left_down = move(pair(0), 2, left, down)
     last = [move(pair(0), 2, left, core)]
+    halos[1].wait_recv()
+    start_if(jnp.logical_not(last_band), to_after)
+    send_states(1)
     halos[0].wait_recv()
-    for copy in halos[1::2]:
-        copy.start()
-    send_states(1)
-    halos[1].wait_recv()
+    start_if(first_band, to_before)
     right_up = move(one(0), 1, right, up)
     right_down = move(one(0), 1, right, down)
     right_x0 = move(one(0), 1, right, across)

time: 108 us -> 108 us (level)
  no operation moved by 1% of the time
where the time goes in v6:
time: 108 us
  Pallas kernels  106 us (98%)
  local copies, waits for them, and re-layouts  2.02 us (2%)
    pallas_call x1, Pallas kernels, body(): pl.pallas_call(kernel, out_shape=jax.ShapeDtypeStruct(states.shape, jnp.b...  106 us

profile of v6, /device:TPU:1, one launch (start us, length us, event | category | flops | bytes accessed | tf_op | source)
XLA Modules:
  0.0 107.8 jit_solution(3963204251665549292)
XLA Ops:
  0.0 105.7 %analysis.1 = bf16[16,131072]{1,0:T(8,128)(2,1)S(1)} custom-call(bf16[16,131072]{1,0:T(8,128)(2,1)} %states.1, bf16[16,4096]{1,0:T(8,128)(2,1)} %obs.1, f32[32,128]{1,0:T(8,128)} %bitcast.2, f32[32,128]{1,0:T(8,128)} %bitcast.3, s32[16,1024]{1,0:T(8,128)} %pick.1, f32[1,1024]{1,0:T(1,128)} %taper.1), custom_call_target="tpu_custom_call" | custom-call | tf_op jit(solution)/shard_map/analysis/pallas_call | solution.py:298
  105.8 2.0 %copy.8 = bf16[16,131072]{1,0:T(8,128)(2,1)} copy(bf16[16,131072]{1,0:T(8,128)(2,1)S(1)} %analysis.1) | data formatting | bytes 8388608

commit v7 on v6

--- a/solution.py
+++ b/solution.py
@@ -26,8 +26,8 @@
 NT = (((1,), (1,)), ((), ()))
 
 PEERS = [
-    (1, 0, 0), (0, 1, 0), (3, 0, 1), (2, 1, 1), (1, 0, 1), (0, 1, 1), (3, 0, 0), (2, 0, 0),
-    (1, 1, 0), (2, 0, 1), (3, 1, 1), (1, 1, 1), (2, 1, 0), (3, 1, 0), (0, 0, 1),
+    (2, 0, 0), (1, 0, 0), (3, 0, 0), (2, 0, 1), (1, 0, 1), (3, 0, 1), (0, 0, 1), (2, 1, 0),
+    (1, 1, 0), (3, 1, 0), (0, 1, 0), (2, 1, 1), (1, 1, 1), (3, 1, 1), (0, 1, 1),
 ]
 
 
@@ -42,7 +42,10 @@
         yy, xx, cc = (y + dy) % 4, (x + dx) % 2, (c + dc) % 2
         return 4 * yy + 2 * xx + cc, 4 * yy + 2 * cc + xx
 
-    peers = [at(*d) for d in PEERS]
+    peers = [
+        tuple(jnp.where(c == 0, first, second) for first, second in zip(at(*a), at(*b)))
+        for a, b in zip(PEERS, PEERS[7:] + PEERS[:7])
+    ]
     before, after = (w + N_WIDE - 1) % N_WIDE, (w + 1) % N_WIDE
     me = 4 * y + 2 * c + x
 

time: 108 us -> 108 us (level)
  no operation moved by 1% of the time
where the time goes in v7:
time: 108 us
  Pallas kernels  106 us (98%)
  local copies, waits for them, and re-layouts  2.02 us (2%)
    pallas_call x1, Pallas kernels, body(): pl.pallas_call(kernel, out_shape=jax.ShapeDtypeStruct(states.shape, jnp.b...  106 us

profile of v7, /device:TPU:1, one launch (start us, length us, event | category | flops | bytes accessed | tf_op | source)
XLA Modules:
  0.0 108.2 jit_solution(13768650940047472358)
XLA Ops:
  0.0 106.1 %analysis.1 = bf16[16,131072]{1,0:T(8,128)(2,1)S(1)} custom-call(bf16[16,131072]{1,0:T(8,128)(2,1)} %states.1, bf16[16,4096]{1,0:T(8,128)(2,1)} %obs.1, f32[32,128]{1,0:T(8,128)} %bitcast.2, f32[32,128]{1,0:T(8,128)} %bitcast.3, s32[16,1024]{1,0:T(8,128)} %pick.1, f32[1,1024]{1,0:T(1,128)} %taper.1), custom_call_target="tpu_custom_call" | custom-call | tf_op jit(solution)/shard_map/analysis/pallas_call | solution.py:301
  106.1 2.0 %copy.8 = bf16[16,131072]{1,0:T(8,128)(2,1)} copy(bf16[16,131072]{1,0:T(8,128)(2,1)S(1)} %analysis.1) | data formatting | bytes 8388608
